TPU v7x, 32 devices: a whole 2x2x4 slice. The times are simulated.
32 devices in a mesh: groups: 2 (over x), radius: 16 (over z, y, core).
Axes of the slice: x: 2, y: 2, z: 4, core: 2. Of those that a mesh axis runs over, the one named last changes fastest.
Arguments:
- states: float32 [8, 400, 2048], P('groups', None, 'radius'), parts along dimension 0, may hold values from -6 to 6
- dipole: float32 [400, 400], replicated, may hold values from -0.625 to 0.625
- pattern: int32 [25, 25], replicated, may hold values 0 or 1
- angular: int32 [400], replicated, may hold values from 0 to 11
- thresholds: float32 [400], replicated, may hold values from 0 to 2
- surface_profile: float32 [2, 2048], P(None, 'radius'), may hold values from 0.2 to 1.5
- pulse_field: float32 [4], P('groups'), parts along dimension 0, may hold values from -0.05 to 0.05
Outputs:
- final_states: float32 [8, 400, 2048], P('groups', None, 'radius'), parts along dimension 0
- gradient: float32 [4], P('groups'), parts along dimension 0
There are 2 independent parts, one for each index of `groups`. A program takes and returns all parts, laid end to end along the dimension named above; an argument that names none is the same for every part. Nothing has to cross between parts.
All inputs are finite; a program needn't handle non-finite values.
Results may differ from a plain program's by a relative error of at most 0.00019.
Values sent between devices are 32-bit elements; how exact they have to be, the bound alone decides.
A program may use at most 64 MiB of HBM per device.

v0:
```python
import functools
import math

import jax
import jax.numpy as jnp
from jax import lax
from jax.experimental import pallas as pl
from jax.experimental.pallas import tpu as pltpu
from jax.sharding import PartitionSpec as P

STEPS = 2
ORDER = 4
inner_radius = 20.0
spacing = 0.08
time_step = 0.005

HALO = 2 * ORDER * STEPS
STRIP = HALO + 2
BASE = 20
ROWS = 16
CHUNKS = 13
BLOCK = 128
AGAIN = 18
GROUP = 5
TREE = (4, 2, 1)
MESH = pl.DeviceIdType.MESH
F32 = jnp.float32
BF16 = jnp.bfloat16


def halves(value):
    high = value.astype(BF16)
    return high, (value - high.astype(F32)).astype(BF16)


def build_coupling(channels, dipole, pattern, chan, square, joined, columns, lhs):
    blocks = pattern.shape[0]
    parts = square.shape[0] // BLOCK
    owned = channels // blocks
    square[...] = jnp.zeros_like(square)
    square[0:channels, 0:channels] = dipole[...]
    joined[...] = jnp.zeros_like(joined)
    joined[0:blocks, 0:blocks] = pattern[...].astype(F32)
    either = jnp.maximum(joined[...], joined[...].T).astype(BF16)
    lane = lax.broadcasted_iota(jnp.int32, (BLOCK, BLOCK), 1)
    row = lax.broadcasted_iota(jnp.int32, (BLOCK, BLOCK), 0)

    def pick(part):
        return jnp.where((row + part * BLOCK) // owned == lane, 1.0, 0.0).astype(BF16)

    def spread(which, part):
        return jnp.broadcast_to(chan[which : which + 1, part * BLOCK : (part + 1) * BLOCK], (BLOCK, BLOCK))

    across = [spread(0, part) for part in range(parts)]
    picks = [pick(part) for part in range(parts)]
    for i in range(parts):
        down = across[i].T
        rows = slice(i * BLOCK, (i + 1) * BLOCK)
        columns[0, rows, :] = spread(1, i).T
        columns[1, rows, :] = 0.5 * (down * (down + 1.0))
        held = jnp.dot(picks[i], either, preferred_element_type=F32).astype(BF16)
        found = {}
        for j in range(parts):
            cols = slice(j * BLOCK, (j + 1) * BLOCK)
            mask = lax.dot_general(held, picks[j], (((1,), (1,)), ((), ())), preferred_element_type=F32)
            allowed = (mask > 0.5) & (jnp.abs(down - across[j]) == 1.0)
            mean = 0.5 * (square[rows, cols] + square[cols, rows].T)
            coupling = jnp.where(allowed, mean, 0.0)
            high = coupling.astype(BF16).astype(F32)
            rest = coupling - high
            for copy, value in enumerate((high, high, rest)):
                place = copy * channels + j * BLOCK
                tile, off = place // BLOCK, place % BLOCK
                moved = pltpu.roll(value, off, 1) if off else value
                for tile, kept in ((tile, lane >= off), (tile + 1, lane < off)):
                    if tile in found:
                        found[tile] = found[tile] + jnp.where(kept, moved, 0.0)
                    elif tile < lhs.shape[1] // BLOCK:
                        found[tile] = jnp.where(kept, moved, 0.0)
        for tile, value in found.items():
            lhs[rows, tile * BLOCK : (tile + 1) * BLOCK] = value.astype(BF16)


def kernel(
    count, channels, states_in, dipole_in, pattern_in, angular_in, thresholds_in, prof_in, pulse, out, grad,
    to_left, to_right, from_left, from_right, strip,
    term, total, rhs, mixed, bound, surface, pot, partial, gathered,
    lhs, square, joined, columns, states, dipole, pattern, angular, thresholds, chan, prof, load,
    halo_send, halo_recv, strip_send, strip_recv, grad_send, grad_recv,
):
    me = lax.axis_index("radius")
    size = 128
    has_left, has_right = me > 0, me < count - 1
    lane = lax.broadcasted_iota(jnp.int32, (ROWS, size), 1)
    row_lane = lane[0:1, :]
    extra_rows = 16
    loads = [
        pltpu.make_async_copy(source, target, load.at[which])
        for which, (source, target) in enumerate(
            ((states_in, states), (prof_in, prof), (dipole_in, dipole), (pattern_in, pattern), (angular_in, angular), (thresholds_in, thresholds))
        )
    ]
    for copy in loads:
        copy.start()

    def over_rows(body, carry=0):
        def several(index, carry):
            for part in range(GROUP):
                carry = body(pl.multiple_of((index * GROUP + part) * ROWS, ROWS), carry)
            return carry

        return lax.fori_loop(0, channels // ROWS // GROUP, several, carry)

    barrier = pltpu.get_barrier_semaphore()

    def greet(d, _):
        other = lax.rem(me + d, count)
        pl.semaphore_signal(barrier, inc=1, device_id={"radius": other}, device_id_type=MESH)
        return 0

    lax.fori_loop(1, count, greet, 0)

    loads[0].wait()
    loads[1].wait()
    low = lane < 64
    low_quarter = lax.rem(lane, 64) < 32
    padded_prof = jnp.concatenate([prof[...], jnp.zeros((extra_rows - 2, size), F32)], axis=0)
    turned_prof = pltpu.roll(padded_prof, 64, 1)

    def pack(rows, parts):
        a, b, c, d = parts
        left = jnp.where(low_quarter, jnp.where(low, a, b), pltpu.roll(jnp.where(low, c, d), 32, 1))
        right = jnp.where(low_quarter, pltpu.roll(jnp.where(low, d, c), 96, 1), jnp.where(low, b, a))
        to_left[rows, :] = left
        to_right[rows, :] = right

    def pack_rows(start, carry):
        rows = pl.ds(start, ROWS)
        a, c = states[0, rows, :], states[2, rows, :]
        b, d = pltpu.roll(states[1, rows, :], 64, 1), pltpu.roll(states[3, rows, :], 64, 1)
        pack(rows, (a, b, c, d))
        for pair, (first, other) in enumerate(((a, b), (c, d))):
            term[pair, rows, 0:size] = first
            term[pair, rows, size : 2 * size] = other
        return carry

    over_rows(pack_rows)
    pack(slice(channels, channels + extra_rows), (padded_prof, turned_prof, padded_prof, turned_prof))

    @pl.when(me == 0)
    def _():
        strip[...] = to_left[...]

    pl.semaphore_wait(barrier, count - 1)

    def halo_copy(source, target, which, other):
        return pltpu.make_async_remote_copy(
            src_ref=source, dst_ref=target, send_sem=halo_send.at[which],
            recv_sem=halo_recv.at[which], device_id={"radius": other}, device_id_type=MESH,
        )

    left_copy = halo_copy(to_left, from_right, 0, jnp.maximum(me - 1, 0))
    right_copy = halo_copy(to_right, from_left, 1, jnp.minimum(me + 1, count - 1))

    chunk = (channels + extra_rows) // CHUNKS
    children = []
    for step in TREE:
        child = me + step
        mine = (lax.rem(me, 2 * step) == 0) if step < TREE[0] else (lax.rem(me, step) == 0)
        children.append((child, mine & (child < count)))

    def strip_copy(part, which):
        rows = pl.ds(part * chunk, chunk)
        return pltpu.make_async_remote_copy(
            src_ref=strip.at[rows, :], dst_ref=strip.at[rows, :],
            send_sem=strip_send.at[which, part], recv_sem=strip_recv.at[part],
            device_id={"radius": jnp.minimum(children[which][0], count - 1)}, device_id_type=MESH,
        )

    def send_on(part):
        for which in range(len(TREE)):
            @pl.when(children[which][1])
            def _():
                strip_copy(part, which).start()

    @pl.when(me == 0)
    def _():
        for part in range(CHUNKS):
            send_on(part)

    @pl.when(has_left)
    def _():
        left_copy.start()

    @pl.when(has_right)
    def _():
        right_copy.start()

    for copy in loads[2:]:
        copy.wait()
    chan[...] = jnp.zeros_like(chan)
    chan[0:1, 0:channels] = angular[...].astype(F32)
    chan[1:2, 0:channels] = thresholds[...]
    build_coupling(channels, dipole, pattern, chan, square, joined, columns, lhs)

    @pl.when(me > 0)
    def _():
        for part in range(CHUNKS):
            strip_copy(part, 0).wait_recv()
            send_on(part)

    second = (lane >= 48) & (lane < 112)
    place = jnp.where(second, lax.rem(lane + 64, size), lane)
    in_right, in_left = place < HALO, place >= size - HALO
    in_strip = (place >= BASE) & (place < BASE + STRIP)
    here = me * size
    extra = jnp.where(in_right, here + size + place, jnp.where(in_left, here - size + place, place - BASE))
    valid = (in_right & has_right) | (in_left & has_left) | in_strip
    extra = jnp.where(valid, extra, 0)
    keep = jnp.where(valid, 1.0, 0.0).astype(F32)
    flip = jnp.where(second, -keep, keep)
    positions = jnp.concatenate([here + row_lane, here + lax.rem(row_lane + 64, size), extra[0:1, :]], axis=1)
    radial = inner_radius + (positions + 1).astype(F32) * spacing
    inverse = 1.0 / (radial * radial)

    @pl.when(has_right)
    def _():
        left_copy_in = halo_copy(to_left, from_right, 0, jnp.minimum(me + 1, count - 1))
        left_copy_in.wait_recv()

    @pl.when(jnp.logical_not(has_right))
    def _():
        from_right[...] = jnp.zeros_like(from_right)

    @pl.when(has_left)
    def _():
        right_copy_in = halo_copy(to_right, from_left, 1, jnp.maximum(me - 1, 0))
        right_copy_in.wait_recv()

    @pl.when(jnp.logical_not(has_left))
    def _():
        from_left[...] = jnp.zeros_like(from_left)

    def unpack(cut, pair):
        right, left, inner = from_right[cut, :], from_left[cut, :], strip[cut, :]
        if pair == 1:
            right, left = pltpu.roll(right, 96, 1), pltpu.roll(left, 32, 1)
        inner = pltpu.roll(inner, BASE if pair == 0 else BASE + 96, 1)
        found = jnp.where(in_right, right, jnp.where(in_left, left, inner))
        return jnp.where(valid, found, 0.0)

    def shift(value, amount):
        return pltpu.roll(value, amount % size, 1)

    def wide(pair, tile):
        first = 4 * size + pair * size if tile == 2 else 2 * pair * size + tile * size
        return slice(first, first + size)

    near = (lax.rem(lane, 64) >= BASE) & (lax.rem(lane, 64) < BASE + 4)

    def store_tile(pair, tile, start, value):
        cols = wide(pair, tile)
        high, rest = halves(value)
        if tile == 2:
            again = pltpu.roll(jnp.where(near, high.astype(F32), 0.0), AGAIN, 1)
            high = (high.astype(F32) + again).astype(BF16)
        rhs[pl.ds(start, ROWS), cols] = high
        rhs[pl.ds(channels + start, ROWS), cols] = rest
        rhs[pl.ds(2 * channels + start, ROWS), cols] = high

    def store_split(pair, start, tiles):
        for tile, value in enumerate(tiles):
            store_tile(pair, tile, start, value)

    unit = 0.5 / (spacing * spacing) / 12.0
    prof_extra = unpack(slice(channels, channels + extra_rows), 0)
    prof_all = jnp.concatenate([padded_prof, turned_prof, prof_extra], axis=1)
    row = lax.broadcasted_iota(jnp.int32, (size, 1), 0)
    spot = lax.rem(row, 64)
    again = (spot >= BASE + AGAIN) & (spot < BASE + AGAIN + 4)
    point = spot - BASE
    def weights(values):
        found = jnp.zeros((size, 1), F32)
        for index, value in enumerate(values):
            found = jnp.where(point == index, value / unit, found)
        return found

    value_weight = weights((4.0, -6.0, 4.0, -1.0))
    slope_weight = weights((-13.0 / 3.0, 9.5, -7.0, 11.0 / 6.0))
    owner = jnp.concatenate([jnp.zeros((1, size), jnp.int32), jnp.ones((1, size), jnp.int32), jnp.where(second, 1, 0)[0:1, :]], axis=1)
    full = value_weight * prof_all[0:1, :] + slope_weight * prof_all[1:2, :]
    full = jnp.where((row // 64) == owner, full, 0.0)

    def chain(index):
        tile, at = index // size, lax.rem(index, size)
        half = lax.rem(at + 64, size)
        other = (at >= 48) & (at < 112)
        spot = jnp.where(other, half, at)
        place = jnp.where(spot < HALO, spot + size, jnp.where(spot >= size - HALO, spot - size, 1000 + spot))
        inside = (spot < BASE + STRIP) | (spot >= size - HALO)
        inside = inside & ((spot < HALO) | (spot >= BASE))
        place = jnp.where(inside, place + jnp.where(other, 4000, 0), 10000 + 10 * at)
        return jnp.where(tile == 0, at, jnp.where(tile == 1, 4000 + half, place))

    across = chain(lax.broadcasted_iota(jnp.int32, (1, 3 * size), 1))
    for tile in range(3):
        down = chain(row + tile * size)
        apart = jnp.abs(down - across)
        band = jnp.where(apart == 2, 1.0, jnp.where(apart == 1, -16.0, 0.0))
        if tile == 2:
            band = band + full
        high = band.astype(BF16)
        if tile == 2:
            low_part = pltpu.roll(band - high.astype(F32), AGAIN, 0)
            high = jnp.where(again, low_part, high.astype(F32)).astype(BF16)
        for copy in range(2):
            first = (3 * copy + tile) * size
            surface[first : first + size, :] = high

    rhs[3 * channels :, :] = jnp.zeros((rhs.shape[0] - 3 * channels, 6 * size), BF16)
    diagonal = 1.25 / (spacing * spacing) / unit

    def begin(start, carry):
        rows = pl.ds(start, ROWS)
        for tile in range(3):
            cols = slice(tile * size, (tile + 1) * size)
            level = columns[0, rows, :] + columns[1, rows, :] * inverse[:, cols]
            pot[rows, cols] = level / unit + diagonal
        for pair in range(2):
            tiles = [term[pair, rows, 0:size], term[pair, rows, size : 2 * size], unpack(rows, pair)]
            term[pair, rows, 2 * size :] = tiles[2]
            store_split(pair, start, tiles)
            total[0, pair, rows, :] = jnp.concatenate(tiles, axis=1)
            total[1, pair, rows, :] = jnp.zeros((ROWS, 3 * size), F32)
        return carry

    over_rows(begin)

    def grad_copy(other, slot):
        return pltpu.make_async_remote_copy(
            src_ref=partial, dst_ref=gathered.at[slot], send_sem=grad_send.at[other],
            recv_sem=grad_recv.at[slot], device_id={"radius": other}, device_id_type=MESH,
        )

    def one_step(step, _):
        strength = pulse[step]
        driven = (strength / unit) * radial

        def one_term(index, _):
            power = index + 1
            scale = unit * time_step / power.astype(F32)
            odd = lax.rem(power, 2)
            signed = jnp.where(odd == 1, -scale, scale)

            stacked = []
            for pair in range(2):
                tiles = [rhs[part : part + channels, wide(pair, tile)] for part in (0, channels) for tile in range(3)]
                stacked.append(jnp.concatenate(tiles, axis=1))
            bound[...] = jnp.dot(jnp.concatenate(stacked, axis=0), surface[...], preferred_element_type=F32)

            def mix(block):
                cols = slice(block * 2 * size, (block + 1) * 2 * size)
                mixed[:, cols] = jnp.dot(lhs[0:channels, :], rhs[:, cols], preferred_element_type=F32)

            mix(0)

            @pl.when(index == 0)
            def _():
                def meet(start, found):
                    rows = pl.ds(start, ROWS)
                    turned = shift(mixed[rows, size : 2 * size], 64) * term[1, rows, 0:size]
                    straight = shift(term[1, rows, size : 2 * size], 64) * mixed[rows, 0:size]
                    both = turned - straight
                    return found + both[0:8] + both[8:16]

                partial[step] = over_rows(meet, jnp.zeros((8, size), F32)) * radial[:, 0:size]

                @pl.when(step == STEPS - 1)
                def _():
                    def send(d, _):
                        grad_copy(lax.rem(me + d, count), me).start()
                        return 0

                    lax.fori_loop(1, count, send, 0)

            def advance(pair, tile):
                cols = slice(tile * size, (tile + 1) * size)
                factor = (signed, -signed, signed * flip)[tile]
                spread_driven = jnp.broadcast_to(driven[:, cols], (ROWS, size))
                for start in range(0, channels, ROWS):
                    rows = slice(start, start + ROWS)
                    value = bound[pair * channels + start : pair * channels + start + ROWS, cols]
                    value = value + pot[rows, cols] * term[pair, rows, cols]
                    value = value + spread_driven * mixed[rows, wide(pair, tile)]
                    value = factor * value
                    term[pair, rows, cols] = value
                    total[odd, pair, rows, cols] += value
                    store_tile(pair, tile, start, value)

            mix(1)
            advance(0, 0)
            advance(0, 1)
            mix(2)
            advance(1, 0)
            advance(1, 1)
            advance(0, 2)
            advance(1, 2)
            return 0

        lax.fori_loop(0, ORDER, one_term, 0)

        def close(start, carry):
            rows = pl.ds(start, ROWS)
            for pair in range(2):
                tiles = []
                for tile in range(3):
                    cols = slice(tile * size, (tile + 1) * size)
                    source = (1, 0, 2)[tile]
                    turned = shift(total[1, pair, rows, source * size : (source + 1) * size], 64)
                    tiles.append(total[0, pair, rows, cols] + turned)
                for tile in range(3):
                    cols = slice(tile * size, (tile + 1) * size)
                    term[pair, rows, cols] = tiles[tile]
                    total[0, pair, rows, cols] = tiles[tile]
                    total[1, pair, rows, cols] = jnp.zeros((ROWS, size), F32)
                store_split(pair, start, tiles)
            return carry

        over_rows(close)
        return 0

    lax.fori_loop(0, STEPS, one_step, 0)

    def finish_rows(start, carry):
        rows = pl.ds(start, ROWS)
        for pair in range(2):
            out[2 * pair, rows, :] = term[pair, rows, 0:size]
            out[2 * pair + 1, rows, :] = shift(term[pair, rows, size : 2 * size], 64)
        return carry

    over_rows(finish_rows)

    gathered[me] = partial[...]

    def collect(d, _):
        other = lax.rem(me + d, count)
        copy = grad_copy(other, other)
        copy.wait_recv()
        return 0

    lax.fori_loop(1, count, collect, 0)
    normalizer = math.sqrt(channels * count * size) * (inner_radius + count * size * spacing)
    for step in range(STEPS):
        found = jnp.zeros((8, size), F32)
        for index in range(count):
            found = found + gathered[index, step]
        grad[step] = jnp.sum(found) / normalizer

    def finish(d, _):
        grad_copy(lax.rem(me + d, count), me).wait_send()
        return 0

    lax.fori_loop(1, count, finish, 0)

    @pl.when(has_left)
    def _():
        left_copy.wait_send()

    @pl.when(has_right)
    def _():
        right_copy.wait_send()

    for which in range(len(TREE)):
        @pl.when(children[which][1])
        def _():
            for part in range(CHUNKS):
                strip_copy(part, which).wait_send()


def per_device(count, states, dipole, pattern, angular, thresholds, surface_profile, pulse_field):
    channels = states.shape[1]
    size = states.shape[2]
    padded = -(-channels // BLOCK) * BLOCK
    depth = -(-3 * channels // 256) * 256
    angular, thresholds = angular[None, :], thresholds[None, :]
    vmem = pl.BlockSpec(memory_space=pltpu.VMEM)
    smem = pl.BlockSpec(memory_space=pltpu.SMEM)
    message = pltpu.VMEM((channels + 16, size), F32)
    wide = (2, channels, 3 * size)
    return pl.pallas_call(
        functools.partial(kernel, count, channels),
        out_shape=(
            jax.ShapeDtypeStruct(states.shape, F32),
            jax.ShapeDtypeStruct(pulse_field.shape, F32),
        ),
        in_specs=[pl.BlockSpec(memory_space=pl.ANY)] * 6 + [smem],
        out_specs=(vmem, smem),
        scratch_shapes=[
            message, message, message, message, message,
            pltpu.VMEM(wide, F32),
            pltpu.VMEM((2,) + wide, F32),
            pltpu.VMEM((depth, 6 * size), BF16),
            pltpu.VMEM((channels, 6 * size), F32),
            pltpu.VMEM((2 * channels, 3 * size), F32),
            pltpu.VMEM((6 * size, 3 * size), BF16),
            pltpu.VMEM((channels, 3 * size), F32),
            pltpu.VMEM((STEPS, 8, size), F32),
            pltpu.VMEM((count, STEPS, 8, size), F32),
            pltpu.VMEM((padded, depth), BF16),
            pltpu.VMEM((padded, padded), F32),
            pltpu.VMEM((BLOCK, BLOCK), F32),
            pltpu.VMEM((2, padded, BLOCK), F32),
            pltpu.VMEM(states.shape, F32),
            pltpu.VMEM(dipole.shape, F32),
            pltpu.VMEM(pattern.shape, jnp.int32),
            pltpu.VMEM(angular.shape, jnp.int32),
            pltpu.VMEM(thresholds.shape, F32),
            pltpu.VMEM((8, padded), F32),
            pltpu.VMEM(surface_profile.shape, F32),
            pltpu.SemaphoreType.DMA((6,)),
            pltpu.SemaphoreType.DMA((2,)),
            pltpu.SemaphoreType.DMA((2,)),
            pltpu.SemaphoreType.DMA((len(TREE), CHUNKS)),
            pltpu.SemaphoreType.DMA((CHUNKS,)),
            pltpu.SemaphoreType.DMA((count,)),
            pltpu.SemaphoreType.DMA((count,)),
        ],
        compiler_params=pltpu.CompilerParams(
            collective_id=0, has_side_effects=True, vmem_limit_bytes=63 * 1024 * 1024
        ),
        cost_estimate=pl.CostEstimate(flops=8000000000, bytes_accessed=4000000, transcendentals=0),
    )(states, dipole, pattern, angular, thresholds, surface_profile, pulse_field)


def solution(mesh):
    return jax.shard_map(
        functools.partial(per_device, mesh.shape["radius"]),
        mesh=mesh,
        in_specs=(P("groups", None, "radius"), P(), P(), P(), P(), P(None, "radius"), P("groups")),
        out_specs=(P("groups", None, "radius"), P("groups")),
        check_vma=False,
    )
```

profile of v0, /device:TPU:29, one launch (start us, length us, event | category | flops | bytes accessed | tf_op | source)
XLA Modules:
  0.0 48.2 jit_solution(9797076138197767930)
XLA Ops:
  0.6 45.0 %shard_map.86 = (f32[4,400,128]{2,1,0:T(8,128)}, f32[2]{0:T(128)}) custom-call(f32[4,400,128]{2,1,0:T(8,128)} %states_in.1, f32[400,400]{1,0:T(8,128)} %dipole_in.1, s32[25,25]{1,0:T(8,128)} %pattern_in.1, s32[1,400]{1,0:T(1,128)} %bitcast.2, f32[1,400]{1,0:T(1,128)} %bitcast.3, f32[2,128]{1,0:T(2,128)} %prof_in.1, f32[2]{0:T(128)} %pulse.1), custom_call_target="tpu_custom_call" | custom-call | flops 8000000000 | bytes 4000000 | tf_op jit(solution)/shard_map/pallas_call | solution.py:490
  45.6 0.0 copy-start
  45.6 2.1 %copy.11 = f32[4,400,128]{2,1,0:T(8,128)} copy(f32[4,400,128]{2,1,0:T(8,128)} %get-tuple-element.4) | data formatting | bytes 1638400
  47.7 0.0 copy-done
  47.7 0.5 %copy.12 = f32[2]{0:T(128)} copy(f32[2]{0:T(128)S(1)} %copy-done) | data formatting | bytes 16
Async XLA Ops:
  45.6 2.1 %copy-start = (f32[2]{0:T(128)S(1)}, f32[2]{0:T(128)}, u32[]{:S(2)}) copy-start(f32[2]{0:T(128)} %get-tuple-element.5) | copy-start | bytes 28
where the time goes:
time: 48.4 us; the launch traced here: 48.2 us
  Pallas kernels  45 us (93%)
  local copies, waits for them, and re-layouts  2.6 us (5%)
  between operations  0.65 us (1%)
    pallas_call x1, Pallas kernels, per_device(): pl.pallas_call(functools.partial(kernel, count, channels), out_shape=(jax...  45 us
    unnamed x4, local copies, waits for them, and re-layouts  2.6 us

commit v1 on v0

--- a/solution.py
+++ b/solution.py
@@ -18,7 +18,7 @@
 STRIP = HALO + 2
 BASE = 20
 ROWS = 16
-CHUNKS = 13
+CHUNKS = 4
 BLOCK = 128
 AGAIN = 18
 GROUP = 5
@@ -45,25 +45,29 @@
     lane = lax.broadcasted_iota(jnp.int32, (BLOCK, BLOCK), 1)
     row = lax.broadcasted_iota(jnp.int32, (BLOCK, BLOCK), 0)
 
-    def pick(part):
-        return jnp.where((row + part * BLOCK) // owned == lane, 1.0, 0.0).astype(BF16)
+    def pick(place, block):
+        first = block * owned
+        return jnp.where((place >= first) & (place < first + owned), 1.0, 0.0).astype(BF16)
 
     def spread(which, part):
         return jnp.broadcast_to(chan[which : which + 1, part * BLOCK : (part + 1) * BLOCK], (BLOCK, BLOCK))
 
     across = [spread(0, part) for part in range(parts)]
-    picks = [pick(part) for part in range(parts)]
+    picks = pick(
+        lax.broadcasted_iota(jnp.int32, (BLOCK, parts * BLOCK), 1),
+        lax.broadcasted_iota(jnp.int32, (BLOCK, parts * BLOCK), 0),
+    )
     for i in range(parts):
         down = across[i].T
         rows = slice(i * BLOCK, (i + 1) * BLOCK)
         columns[0, rows, :] = spread(1, i).T
         columns[1, rows, :] = 0.5 * (down * (down + 1.0))
-        held = jnp.dot(picks[i], either, preferred_element_type=F32).astype(BF16)
+        held = jnp.dot(pick(row + i * BLOCK, lane), either, preferred_element_type=F32).astype(BF16)
+        masks = jnp.dot(held, picks, preferred_element_type=F32)
         found = {}
         for j in range(parts):
             cols = slice(j * BLOCK, (j + 1) * BLOCK)
-            mask = lax.dot_general(held, picks[j], (((1,), (1,)), ((), ())), preferred_element_type=F32)
-            allowed = (mask > 0.5) & (jnp.abs(down - across[j]) == 1.0)
+            allowed = (masks[:, cols] > 0.5) & (jnp.abs(down - across[j]) == 1.0)
             mean = 0.5 * (square[rows, cols] + square[cols, rows].T)
             coupling = jnp.where(allowed, mean, 0.0)
             high = coupling.astype(BF16).astype(F32)
@@ -83,7 +87,7 @@
 
 def kernel(
     count, channels, states_in, dipole_in, pattern_in, angular_in, thresholds_in, prof_in, pulse, out, grad,
-    to_left, to_right, from_left, from_right, strip,
+    to_left, to_right, from_left, from_right, strip, left_half, right_half, left_in, right_in,
     term, total, rhs, mixed, bound, surface, pot, partial, gathered,
     lhs, square, joined, columns, states, dipole, pattern, angular, thresholds, chan, prof, load,
     halo_send, halo_recv, strip_send, strip_recv, grad_send, grad_recv,
@@ -123,7 +127,7 @@
     loads[0].wait()
     loads[1].wait()
     low = lane < 64
-    low_quarter = lax.rem(lane, 64) < 32
+    low_quarter = (lane & 63) < 32
     padded_prof = jnp.concatenate([prof[...], jnp.zeros((extra_rows - 2, size), F32)], axis=0)
     turned_prof = pltpu.roll(padded_prof, 64, 1)
 
@@ -151,6 +155,20 @@
     def _():
         strip[...] = to_left[...]
 
+    message = (channels + extra_rows) // 2
+    first_half = (lane & 31) < HALO
+
+    def squeeze(index, _):
+        near_rows = pl.ds(pl.multiple_of(index * ROWS, ROWS), ROWS)
+        far_rows = pl.ds(pl.multiple_of(message + index * ROWS, ROWS), ROWS)
+        left_half[near_rows, :] = jnp.where(first_half, to_left[near_rows, :], pltpu.roll(to_left[far_rows, :], HALO, 1))
+        right_half[near_rows, :] = jnp.where(
+            first_half, pltpu.roll(to_right[far_rows, :], size - HALO, 1), to_right[near_rows, :]
+        )
+        return 0
+
+    lax.fori_loop(0, message // ROWS, squeeze, 0)
+
     pl.semaphore_wait(barrier, count - 1)
 
     def halo_copy(source, target, which, other):
@@ -159,8 +177,8 @@
             recv_sem=halo_recv.at[which], device_id={"radius": other}, device_id_type=MESH,
         )
 
-    left_copy = halo_copy(to_left, from_right, 0, jnp.maximum(me - 1, 0))
-    right_copy = halo_copy(to_right, from_left, 1, jnp.minimum(me + 1, count - 1))
+    left_copy = halo_copy(left_half, right_in, 0, jnp.maximum(me - 1, 0))
+    right_copy = halo_copy(right_half, left_in, 1, jnp.minimum(me + 1, count - 1))
 
     chunk = (channels + extra_rows) // CHUNKS
     children = []
@@ -201,16 +219,26 @@
     chan[...] = jnp.zeros_like(chan)
     chan[0:1, 0:channels] = angular[...].astype(F32)
     chan[1:2, 0:channels] = thresholds[...]
-    build_coupling(channels, dipole, pattern, chan, square, joined, columns, lhs)
-
-    @pl.when(me > 0)
-    def _():
-        for part in range(CHUNKS):
-            strip_copy(part, 0).wait_recv()
-            send_on(part)
+    pass_first = (lax.rem(me, TREE[0]) == 0) & (me > 0) & (me <= count // 2)
+    build_phase = jnp.where(pass_first, 1, 0)
+
+    def phase(which, _):
+        @pl.when(which == build_phase)
+        def _():
+            build_coupling(channels, dipole, pattern, chan, square, joined, columns, lhs)
+
+        @pl.when((which != build_phase) & (me > 0))
+        def _():
+            for part in range(CHUNKS):
+                strip_copy(part, 0).wait_recv()
+                send_on(part)
+
+        return 0
+
+    lax.fori_loop(0, 2, phase, 0)
 
     second = (lane >= 48) & (lane < 112)
-    place = jnp.where(second, lax.rem(lane + 64, size), lane)
+    place = jnp.where(second, ((lane + 64) & (size - 1)), lane)
     in_right, in_left = place < HALO, place >= size - HALO
     in_strip = (place >= BASE) & (place < BASE + STRIP)
     here = me * size
@@ -219,27 +247,39 @@
     extra = jnp.where(valid, extra, 0)
     keep = jnp.where(valid, 1.0, 0.0).astype(F32)
     flip = jnp.where(second, -keep, keep)
-    positions = jnp.concatenate([here + row_lane, here + lax.rem(row_lane + 64, size), extra[0:1, :]], axis=1)
+    positions = jnp.concatenate([here + row_lane, here + ((row_lane + 64) & (size - 1)), extra[0:1, :]], axis=1)
     radial = inner_radius + (positions + 1).astype(F32) * spacing
     inverse = 1.0 / (radial * radial)
 
     @pl.when(has_right)
     def _():
-        left_copy_in = halo_copy(to_left, from_right, 0, jnp.minimum(me + 1, count - 1))
+        left_copy_in = halo_copy(left_half, right_in, 0, jnp.minimum(me + 1, count - 1))
         left_copy_in.wait_recv()
 
     @pl.when(jnp.logical_not(has_right))
     def _():
-        from_right[...] = jnp.zeros_like(from_right)
+        right_in[...] = jnp.zeros_like(right_in)
 
     @pl.when(has_left)
     def _():
-        right_copy_in = halo_copy(to_right, from_left, 1, jnp.maximum(me - 1, 0))
+        right_copy_in = halo_copy(right_half, left_in, 1, jnp.maximum(me - 1, 0))
         right_copy_in.wait_recv()
 
     @pl.when(jnp.logical_not(has_left))
     def _():
-        from_left[...] = jnp.zeros_like(from_left)
+        left_in[...] = jnp.zeros_like(left_in)
+
+    def stretch(index, _):
+        near_rows = pl.ds(pl.multiple_of(index * ROWS, ROWS), ROWS)
+        far_rows = pl.ds(pl.multiple_of(message + index * ROWS, ROWS), ROWS)
+        right, left = right_in[near_rows, :], left_in[near_rows, :]
+        from_right[near_rows, :] = right
+        from_right[far_rows, :] = pltpu.roll(right, size - HALO, 1)
+        from_left[near_rows, :] = left
+        from_left[far_rows, :] = pltpu.roll(left, HALO, 1)
+        return 0
+
+    lax.fori_loop(0, message // ROWS, stretch, 0)
 
     def unpack(cut, pair):
         right, left, inner = from_right[cut, :], from_left[cut, :], strip[cut, :]
@@ -256,7 +296,7 @@
         first = 4 * size + pair * size if tile == 2 else 2 * pair * size + tile * size
         return slice(first, first + size)
 
-    near = (lax.rem(lane, 64) >= BASE) & (lax.rem(lane, 64) < BASE + 4)
+    near = ((lane & 63) >= BASE) & ((lane & 63) < BASE + 4)
 
     def store_tile(pair, tile, start, value):
         cols = wide(pair, tile)
@@ -276,7 +316,7 @@
     prof_extra = unpack(slice(channels, channels + extra_rows), 0)
     prof_all = jnp.concatenate([padded_prof, turned_prof, prof_extra], axis=1)
     row = lax.broadcasted_iota(jnp.int32, (size, 1), 0)
-    spot = lax.rem(row, 64)
+    spot = row & 63
     again = (spot >= BASE + AGAIN) & (spot < BASE + AGAIN + 4)
     point = spot - BASE
     def weights(values):
@@ -289,11 +329,11 @@
     slope_weight = weights((-13.0 / 3.0, 9.5, -7.0, 11.0 / 6.0))
     owner = jnp.concatenate([jnp.zeros((1, size), jnp.int32), jnp.ones((1, size), jnp.int32), jnp.where(second, 1, 0)[0:1, :]], axis=1)
     full = value_weight * prof_all[0:1, :] + slope_weight * prof_all[1:2, :]
-    full = jnp.where((row // 64) == owner, full, 0.0)
+    full = jnp.where((row >> 6) == owner, full, 0.0)
 
     def chain(index):
-        tile, at = index // size, lax.rem(index, size)
-        half = lax.rem(at + 64, size)
+        tile, at = index >> 7, index & (size - 1)
+        half = (at + 64) & (size - 1)
         other = (at >= 48) & (at < 112)
         spot = jnp.where(other, half, at)
         place = jnp.where(spot < HALO, spot + size, jnp.where(spot >= size - HALO, spot - size, 1000 + spot))
@@ -486,6 +526,7 @@
     vmem = pl.BlockSpec(memory_space=pltpu.VMEM)
     smem = pl.BlockSpec(memory_space=pltpu.SMEM)
     message = pltpu.VMEM((channels + 16, size), F32)
+    half = pltpu.VMEM(((channels + 16) // 2, size), F32)
     wide = (2, channels, 3 * size)
     return pl.pallas_call(
         functools.partial(kernel, count, channels),
@@ -493,10 +534,10 @@
             jax.ShapeDtypeStruct(states.shape, F32),
             jax.ShapeDtypeStruct(pulse_field.shape, F32),
         ),
-        in_specs=[pl.BlockSpec(memory_space=pl.ANY)] * 6 + [smem],
+        in_specs=[pl.BlockSpec(memory_space=pltpu.HBM)] * 6 + [smem],
         out_specs=(vmem, smem),
         scratch_shapes=[
-            message, message, message, message, message,
+            message, message, message, message, message, half, half, half, half,
             pltpu.VMEM(wide, F32),
             pltpu.VMEM((2,) + wide, F32),
             pltpu.VMEM((depth, 6 * size), BF16),

time: 48.4 us -> 50.3 us (1.039)
  Pallas kernels: 45 us -> 46.9 us
    pallas_call x1, Pallas kernels: 45 us -> 46.9 us  [per_device(): pl.pallas_call(functools.partial(kernel, count, channels), out_shape=(jax...]
where the time goes in v1:
time: 50.3 us; the launch traced here: 50.1 us
  Pallas kernels  46.9 us (93%)
  local copies, waits for them, and re-layouts  2.6 us (5%)
  between operations  0.65 us (1%)
    pallas_call x1, Pallas kernels, per_device(): pl.pallas_call(functools.partial(kernel, count, channels), out_shape=(jax...  46.9 us
    unnamed x4, local copies, waits for them, and re-layouts  2.6 us

profile of v1, /device:TPU:29, one launch (start us, length us, event | category | flops | bytes accessed | tf_op | source)
XLA Modules:
  0.0 50.1 jit_solution(9179221233231320840)
XLA Ops:
  0.6 46.9 %shard_map.86 = (f32[4,400,128]{2,1,0:T(8,128)}, f32[2]{0:T(128)}) custom-call(f32[4,400,128]{2,1,0:T(8,128)} %states_in.1, f32[400,400]{1,0:T(8,128)} %dipole_in.1, s32[25,25]{1,0:T(8,128)} %pattern_in.1, s32[1,400]{1,0:T(1,128)} %bitcast.2, f32[1,400]{1,0:T(1,128)} %bitcast.3, f32[2,128]{1,0:T(2,128)} %prof_in.1, f32[2]{0:T(128)} %pulse.1), custom_call_target="tpu_custom_call" | custom-call | flops 8000000000 | bytes 4000000 | tf_op jit(solution)/shard_map/pallas_call | solution.py:531
  47.5 0.0 copy-start
  47.5 2.1 %copy.11 = f32[4,400,128]{2,1,0:T(8,128)} copy(f32[4,400,128]{2,1,0:T(8,128)} %get-tuple-element.4) | data formatting | bytes 1638400
  49.6 0.0 copy-done
  49.6 0.5 %copy.12 = f32[2]{0:T(128)} copy(f32[2]{0:T(128)S(1)} %copy-done) | data formatting | bytes 16
Async XLA Ops:
  47.5 2.1 %copy-start = (f32[2]{0:T(128)S(1)}, f32[2]{0:T(128)}, u32[]{:S(2)}) copy-start(f32[2]{0:T(128)} %get-tuple-element.5) | copy-start | bytes 28

commit v2 on v1

--- a/solution.py
+++ b/solution.py
@@ -18,7 +18,7 @@
 STRIP = HALO + 2
 BASE = 20
 ROWS = 16
-CHUNKS = 4
+CHUNKS = 13
 BLOCK = 128
 AGAIN = 18
 GROUP = 5
@@ -219,24 +219,6 @@
     chan[...] = jnp.zeros_like(chan)
     chan[0:1, 0:channels] = angular[...].astype(F32)
     chan[1:2, 0:channels] = thresholds[...]
-    pass_first = (lax.rem(me, TREE[0]) == 0) & (me > 0) & (me <= count // 2)
-    build_phase = jnp.where(pass_first, 1, 0)
-
-    def phase(which, _):
-        @pl.when(which == build_phase)
-        def _():
-            build_coupling(channels, dipole, pattern, chan, square, joined, columns, lhs)
-
-        @pl.when((which != build_phase) & (me > 0))
-        def _():
-            for part in range(CHUNKS):
-                strip_copy(part, 0).wait_recv()
-                send_on(part)
-
-        return 0
-
-    lax.fori_loop(0, 2, phase, 0)
-
     second = (lane >= 48) & (lane < 112)
     place = jnp.where(second, ((lane + 64) & (size - 1)), lane)
     in_right, in_left = place < HALO, place >= size - HALO
@@ -251,47 +233,8 @@
     radial = inner_radius + (positions + 1).astype(F32) * spacing
     inverse = 1.0 / (radial * radial)
 
-    @pl.when(has_right)
-    def _():
-        left_copy_in = halo_copy(left_half, right_in, 0, jnp.minimum(me + 1, count - 1))
-        left_copy_in.wait_recv()
-
-    @pl.when(jnp.logical_not(has_right))
-    def _():
-        right_in[...] = jnp.zeros_like(right_in)
-
-    @pl.when(has_left)
-    def _():
-        right_copy_in = halo_copy(right_half, left_in, 1, jnp.maximum(me - 1, 0))
-        right_copy_in.wait_recv()
-
-    @pl.when(jnp.logical_not(has_left))
-    def _():
-        left_in[...] = jnp.zeros_like(left_in)
-
-    def stretch(index, _):
-        near_rows = pl.ds(pl.multiple_of(index * ROWS, ROWS), ROWS)
-        far_rows = pl.ds(pl.multiple_of(message + index * ROWS, ROWS), ROWS)
-        right, left = right_in[near_rows, :], left_in[near_rows, :]
-        from_right[near_rows, :] = right
-        from_right[far_rows, :] = pltpu.roll(right, size - HALO, 1)
-        from_left[near_rows, :] = left
-        from_left[far_rows, :] = pltpu.roll(left, HALO, 1)
-        return 0
-
-    lax.fori_loop(0, message // ROWS, stretch, 0)
-
-    def unpack(cut, pair):
-        right, left, inner = from_right[cut, :], from_left[cut, :], strip[cut, :]
-        if pair == 1:
-            right, left = pltpu.roll(right, 96, 1), pltpu.roll(left, 32, 1)
-        inner = pltpu.roll(inner, BASE if pair == 0 else BASE + 96, 1)
-        found = jnp.where(in_right, right, jnp.where(in_left, left, inner))
-        return jnp.where(valid, found, 0.0)
-
-    def shift(value, amount):
-        return pltpu.roll(value, amount % size, 1)
-
+    unit = 0.5 / (spacing * spacing) / 12.0
+    row = lax.broadcasted_iota(jnp.int32, (size, 1), 0)
     def wide(pair, tile):
         first = 4 * size + pair * size if tile == 2 else 2 * pair * size + tile * size
         return slice(first, first + size)
@@ -311,25 +254,6 @@
     def store_split(pair, start, tiles):
         for tile, value in enumerate(tiles):
             store_tile(pair, tile, start, value)
-
-    unit = 0.5 / (spacing * spacing) / 12.0
-    prof_extra = unpack(slice(channels, channels + extra_rows), 0)
-    prof_all = jnp.concatenate([padded_prof, turned_prof, prof_extra], axis=1)
-    row = lax.broadcasted_iota(jnp.int32, (size, 1), 0)
-    spot = row & 63
-    again = (spot >= BASE + AGAIN) & (spot < BASE + AGAIN + 4)
-    point = spot - BASE
-    def weights(values):
-        found = jnp.zeros((size, 1), F32)
-        for index, value in enumerate(values):
-            found = jnp.where(point == index, value / unit, found)
-        return found
-
-    value_weight = weights((4.0, -6.0, 4.0, -1.0))
-    slope_weight = weights((-13.0 / 3.0, 9.5, -7.0, 11.0 / 6.0))
-    owner = jnp.concatenate([jnp.zeros((1, size), jnp.int32), jnp.ones((1, size), jnp.int32), jnp.where(second, 1, 0)[0:1, :]], axis=1)
-    full = value_weight * prof_all[0:1, :] + slope_weight * prof_all[1:2, :]
-    full = jnp.where((row >> 6) == owner, full, 0.0)
 
     def chain(index):
         tile, at = index >> 7, index & (size - 1)
@@ -343,21 +267,15 @@
         return jnp.where(tile == 0, at, jnp.where(tile == 1, 4000 + half, place))
 
     across = chain(lax.broadcasted_iota(jnp.int32, (1, 3 * size), 1))
-    for tile in range(3):
-        down = chain(row + tile * size)
-        apart = jnp.abs(down - across)
-        band = jnp.where(apart == 2, 1.0, jnp.where(apart == 1, -16.0, 0.0))
-        if tile == 2:
-            band = band + full
-        high = band.astype(BF16)
-        if tile == 2:
-            low_part = pltpu.roll(band - high.astype(F32), AGAIN, 0)
-            high = jnp.where(again, low_part, high.astype(F32)).astype(BF16)
+    def band_rows(tile):
+        apart = jnp.abs(chain(row + tile * size) - across)
+        return jnp.where(apart == 2, 1.0, jnp.where(apart == 1, -16.0, 0.0))
+
+    def store_band(tile, value):
         for copy in range(2):
             first = (3 * copy + tile) * size
-            surface[first : first + size, :] = high
-
-    rhs[3 * channels :, :] = jnp.zeros((rhs.shape[0] - 3 * channels, 6 * size), BF16)
+            surface[first : first + size, :] = value
+
     diagonal = 1.25 / (spacing * spacing) / unit
 
     def begin(start, carry):
@@ -367,14 +285,109 @@
             level = columns[0, rows, :] + columns[1, rows, :] * inverse[:, cols]
             pot[rows, cols] = level / unit + diagonal
         for pair in range(2):
-            tiles = [term[pair, rows, 0:size], term[pair, rows, size : 2 * size], unpack(rows, pair)]
-            term[pair, rows, 2 * size :] = tiles[2]
-            store_split(pair, start, tiles)
-            total[0, pair, rows, :] = jnp.concatenate(tiles, axis=1)
+            for tile in range(2):
+                cols = slice(tile * size, (tile + 1) * size)
+                value = term[pair, rows, cols]
+                store_tile(pair, tile, start, value)
+                total[0, pair, rows, cols] = value
             total[1, pair, rows, :] = jnp.zeros((ROWS, 3 * size), F32)
         return carry
 
-    over_rows(begin)
+    pass_first = (lax.rem(me, TREE[0]) == 0) & (me > 0) & (me <= count // 2)
+    build_phase = jnp.where(pass_first, 1, 0)
+
+    def phase(which, _):
+        @pl.when(which == build_phase)
+        def _():
+            build_coupling(channels, dipole, pattern, chan, square, joined, columns, lhs)
+            for tile in range(2):
+                store_band(tile, band_rows(tile).astype(BF16))
+            rhs[3 * channels :, :] = jnp.zeros((rhs.shape[0] - 3 * channels, 6 * size), BF16)
+            over_rows(begin)
+
+        @pl.when((which != build_phase) & (me > 0))
+        def _():
+            for part in range(CHUNKS):
+                strip_copy(part, 0).wait_recv()
+                send_on(part)
+
+        return 0
+
+    lax.fori_loop(0, 2, phase, 0)
+
+    @pl.when(has_right)
+    def _():
+        left_copy_in = halo_copy(left_half, right_in, 0, jnp.minimum(me + 1, count - 1))
+        left_copy_in.wait_recv()
+
+    @pl.when(jnp.logical_not(has_right))
+    def _():
+        right_in[...] = jnp.zeros_like(right_in)
+
+    @pl.when(has_left)
+    def _():
+        right_copy_in = halo_copy(right_half, left_in, 1, jnp.maximum(me - 1, 0))
+        right_copy_in.wait_recv()
+
+    @pl.when(jnp.logical_not(has_left))
+    def _():
+        left_in[...] = jnp.zeros_like(left_in)
+
+    def stretch(index, _):
+        near_rows = pl.ds(pl.multiple_of(index * ROWS, ROWS), ROWS)
+        far_rows = pl.ds(pl.multiple_of(message + index * ROWS, ROWS), ROWS)
+        right, left = right_in[near_rows, :], left_in[near_rows, :]
+        from_right[near_rows, :] = right
+        from_right[far_rows, :] = pltpu.roll(right, size - HALO, 1)
+        from_left[near_rows, :] = left
+        from_left[far_rows, :] = pltpu.roll(left, HALO, 1)
+        return 0
+
+    lax.fori_loop(0, message // ROWS, stretch, 0)
+
+    def unpack(cut, pair):
+        right, left, inner = from_right[cut, :], from_left[cut, :], strip[cut, :]
+        if pair == 1:
+            right, left = pltpu.roll(right, 96, 1), pltpu.roll(left, 32, 1)
+        inner = pltpu.roll(inner, BASE if pair == 0 else BASE + 96, 1)
+        found = jnp.where(in_right, right, jnp.where(in_left, left, inner))
+        return jnp.where(valid, found, 0.0)
+
+    def shift(value, amount):
+        return pltpu.roll(value, amount % size, 1)
+
+    prof_extra = unpack(slice(channels, channels + extra_rows), 0)
+    prof_all = jnp.concatenate([padded_prof, turned_prof, prof_extra], axis=1)
+    spot = row & 63
+    again = (spot >= BASE + AGAIN) & (spot < BASE + AGAIN + 4)
+    point = spot - BASE
+    def weights(values):
+        found = jnp.zeros((size, 1), F32)
+        for index, value in enumerate(values):
+            found = jnp.where(point == index, value / unit, found)
+        return found
+
+    value_weight = weights((4.0, -6.0, 4.0, -1.0))
+    slope_weight = weights((-13.0 / 3.0, 9.5, -7.0, 11.0 / 6.0))
+    owner = jnp.concatenate([jnp.zeros((1, size), jnp.int32), jnp.ones((1, size), jnp.int32), jnp.where(second, 1, 0)[0:1, :]], axis=1)
+    full = value_weight * prof_all[0:1, :] + slope_weight * prof_all[1:2, :]
+    full = jnp.where((row >> 6) == owner, full, 0.0)
+
+    band = band_rows(2) + full
+    high = band.astype(BF16)
+    low_part = pltpu.roll(band - high.astype(F32), AGAIN, 0)
+    store_band(2, jnp.where(again, low_part, high.astype(F32)).astype(BF16))
+
+    def begin_extra(start, carry):
+        rows = pl.ds(start, ROWS)
+        for pair in range(2):
+            value = unpack(rows, pair)
+            term[pair, rows, 2 * size :] = value
+            total[0, pair, rows, 2 * size :] = value
+            store_tile(pair, 2, start, value)
+        return carry
+
+    over_rows(begin_extra)
 
     def grad_copy(other, slot):
         return pltpu.make_async_remote_copy(

time: 50.3 us -> 49 us (0.974)
  Pallas kernels: 46.9 us -> 45.5 us
    pallas_call x1, Pallas kernels: 46.9 us -> 45.5 us  [per_device(): pl.pallas_call(functools.partial(kernel, count, channels), out_shape=(jax...]
where the time goes in v2:
time: 49 us; the launch traced here: 48.8 us
  Pallas kernels  45.5 us (93%)
  local copies, waits for them, and re-layouts  2.6 us (5%)
  between operations  0.65 us (1%)
    pallas_call x1, Pallas kernels, per_device(): pl.pallas_call(functools.partial(kernel, count, channels), out_shape=(jax...  45.5 us
    unnamed x4, local copies, waits for them, and re-layouts  2.6 us

profile of v2, /device:TPU:29, one launch (start us, length us, event | category | flops | bytes accessed | tf_op | source)
XLA Modules:
  0.0 48.8 jit_solution(5425173466068545187)
XLA Ops:
  0.6 45.5 %shard_map.86 = (f32[4,400,128]{2,1,0:T(8,128)}, f32[2]{0:T(128)}) custom-call(f32[4,400,128]{2,1,0:T(8,128)} %states_in.1, f32[400,400]{1,0:T(8,128)} %dipole_in.1, s32[25,25]{1,0:T(8,128)} %pattern_in.1, s32[1,400]{1,0:T(1,128)} %bitcast.2, f32[1,400]{1,0:T(1,128)} %bitcast.3, f32[2,128]{1,0:T(2,128)} %prof_in.1, f32[2]{0:T(128)} %pulse.1), custom_call_target="tpu_custom_call" | custom-call | flops 8000000000 | bytes 4000000 | tf_op jit(solution)/shard_map/pallas_call | solution.py:544
  46.2 0.0 copy-start
  46.2 2.1 %copy.11 = f32[4,400,128]{2,1,0:T(8,128)} copy(f32[4,400,128]{2,1,0:T(8,128)} %get-tuple-element.4) | data formatting | bytes 1638400
  48.3 0.0 copy-done
  48.3 0.5 %copy.12 = f32[2]{0:T(128)} copy(f32[2]{0:T(128)S(1)} %copy-done) | data formatting | bytes 16
Async XLA Ops:
  46.2 2.1 %copy-start = (f32[2]{0:T(128)S(1)}, f32[2]{0:T(128)}, u32[]{:S(2)}) copy-start(f32[2]{0:T(128)} %get-tuple-element.5) | copy-start | bytes 28

commit v3 on v2

--- a/solution.py
+++ b/solution.py
@@ -158,6 +158,43 @@
     message = (channels + extra_rows) // 2
     first_half = (lane & 31) < HALO
 
+    pl.semaphore_wait(barrier, count - 1)
+
+    def halo_copy(source, target, which, other):
+        return pltpu.make_async_remote_copy(
+            src_ref=source, dst_ref=target, send_sem=halo_send.at[which],
+            recv_sem=halo_recv.at[which], device_id={"radius": other}, device_id_type=MESH,
+        )
+
+    left_copy = halo_copy(left_half, right_in, 0, jnp.maximum(me - 1, 0))
+    right_copy = halo_copy(right_half, left_in, 1, jnp.minimum(me + 1, count - 1))
+
+    chunk = (channels + extra_rows) // CHUNKS
+    children = []
+    for step in TREE:
+        child = me + step
+        mine = (lax.rem(me, 2 * step) == 0) if step < TREE[0] else (lax.rem(me, step) == 0)
+        children.append((child, mine & (child < count)))
+
+    def strip_copy(part, which):
+        rows = pl.ds(part * chunk, chunk)
+        return pltpu.make_async_remote_copy(
+            src_ref=strip.at[rows, :], dst_ref=strip.at[rows, :],
+            send_sem=strip_send.at[which, part], recv_sem=strip_recv.at[part],
+            device_id={"radius": jnp.minimum(children[which][0], count - 1)}, device_id_type=MESH,
+        )
+
+    def send_on(part):
+        for which in range(len(TREE)):
+            @pl.when(children[which][1])
+            def _():
+                strip_copy(part, which).start()
+
+    @pl.when(me == 0)
+    def _():
+        for part in range(CHUNKS):
+            send_on(part)
+
     def squeeze(index, _):
         near_rows = pl.ds(pl.multiple_of(index * ROWS, ROWS), ROWS)
         far_rows = pl.ds(pl.multiple_of(message + index * ROWS, ROWS), ROWS)
@@ -168,43 +205,6 @@
         return 0
 
     lax.fori_loop(0, message // ROWS, squeeze, 0)
-
-    pl.semaphore_wait(barrier, count - 1)
-
-    def halo_copy(source, target, which, other):
-        return pltpu.make_async_remote_copy(
-            src_ref=source, dst_ref=target, send_sem=halo_send.at[which],
-            recv_sem=halo_recv.at[which], device_id={"radius": other}, device_id_type=MESH,
-        )
-
-    left_copy = halo_copy(left_half, right_in, 0, jnp.maximum(me - 1, 0))
-    right_copy = halo_copy(right_half, left_in, 1, jnp.minimum(me + 1, count - 1))
-
-    chunk = (channels + extra_rows) // CHUNKS
-    children = []
-    for step in TREE:
-        child = me + step
-        mine = (lax.rem(me, 2 * step) == 0) if step < TREE[0] else (lax.rem(me, step) == 0)
-        children.append((child, mine & (child < count)))
-
-    def strip_copy(part, which):
-        rows = pl.ds(part * chunk, chunk)
-        return pltpu.make_async_remote_copy(
-            src_ref=strip.at[rows, :], dst_ref=strip.at[rows, :],
-            send_sem=strip_send.at[which, part], recv_sem=strip_recv.at[part],
-            device_id={"radius": jnp.minimum(children[which][0], count - 1)}, device_id_type=MESH,
-        )
-
-    def send_on(part):
-        for which in range(len(TREE)):
-            @pl.when(children[which][1])
-            def _():
-                strip_copy(part, which).start()
-
-    @pl.when(me == 0)
-    def _():
-        for part in range(CHUNKS):
-            send_on(part)
 
     @pl.when(has_left)
     def _():
@@ -293,7 +293,7 @@
             total[1, pair, rows, :] = jnp.zeros((ROWS, 3 * size), F32)
         return carry
 
-    pass_first = (lax.rem(me, TREE[0]) == 0) & (me > 0) & (me <= count // 2)
+    pass_first = me == TREE[0]
     build_phase = jnp.where(pass_first, 1, 0)
 
     def phase(which, _):

time: 49 us -> 49 us (level)
  no operation moved by 1% of the time
where the time goes in v3:
time: 49 us; the launch traced here: 48.8 us
  Pallas kernels  45.5 us (93%)
  local copies, waits for them, and re-layouts  2.6 us (5%)
  between operations  0.65 us (1%)
    pallas_call x1, Pallas kernels, per_device(): pl.pallas_call(functools.partial(kernel, count, channels), out_shape=(jax...  45.5 us
    unnamed x4, local copies, waits for them, and re-layouts  2.6 us

profile of v3, /device:TPU:29, one launch (start us, length us, event | category | flops | bytes accessed | tf_op | source)
XLA Modules:
  0.0 48.8 jit_solution(13500293800555766810)
XLA Ops:
  0.6 45.5 %shard_map.86 = (f32[4,400,128]{2,1,0:T(8,128)}, f32[2]{0:T(128)}) custom-call(f32[4,400,128]{2,1,0:T(8,128)} %states_in.1, f32[400,400]{1,0:T(8,128)} %dipole_in.1, s32[25,25]{1,0:T(8,128)} %pattern_in.1, s32[1,400]{1,0:T(1,128)} %bitcast.2, f32[1,400]{1,0:T(1,128)} %bitcast.3, f32[2,128]{1,0:T(2,128)} %prof_in.1, f32[2]{0:T(128)} %pulse.1), custom_call_target="tpu_custom_call" | custom-call | flops 8000000000 | bytes 4000000 | tf_op jit(solution)/shard_map/pallas_call | solution.py:544
  46.2 0.0 copy-start
  46.2 2.1 %copy.11 = f32[4,400,128]{2,1,0:T(8,128)} copy(f32[4,400,128]{2,1,0:T(8,128)} %get-tuple-element.4) | data formatting | bytes 1638400
  48.3 0.0 copy-done
  48.3 0.5 %copy.12 = f32[2]{0:T(128)} copy(f32[2]{0:T(128)S(1)} %copy-done) | data formatting | bytes 16
Async XLA Ops:
  46.2 2.1 %copy-start = (f32[2]{0:T(128)S(1)}, f32[2]{0:T(128)}, u32[]{:S(2)}) copy-start(f32[2]{0:T(128)} %get-tuple-element.5) | copy-start | bytes 28
